TPU v7x, 128 devices: a whole 4x4x4 slice. The times are simulated.
128 devices in a mesh: tm: 32 (over z, x, y_hi), rows: 4 (over y_lo, core).
Axes of the slice: x: 4, y: 4 (y_hi: 2, y_lo: 2; y = y_hi * 2 + y_lo), z: 4, core: 2. Of those that a mesh axis runs over, the one named last changes fastest.
Arguments:
- video: bfloat16 [256, 32, 128, 128], P('tm', 'rows'), may hold values from -36 to 50
- conv_weight: bfloat16 [3, 3, 3, 128, 256], replicated, may hold values from -0.109375 to 0.109375
- norm_gain: float32 [256], replicated, may hold values from 0.5 to 1.5
- norm_bias: float32 [256], replicated, may hold values from -3 to 3
Outputs:
- patch_tokens: bfloat16 [16, 64, 256, 1024], P('rows', 'tm')
All inputs are finite; a program needn't handle non-finite values.
Results may differ from a plain program's by a relative error of at most 0.0049.
Values may be sent and summed in bfloat16 or wider, within the bound.
A program may use at most 128 MiB of HBM per device.

v0:
```python
import jax
import jax.numpy as jnp
from jax import lax
from jax.sharding import PartitionSpec as P

GROUPS = 32
inv_root = 0.7071067811865476


def from_partner(block, axis, distance):
    count = lax.axis_size(axis)
    route = []
    for low in range(count):
        high = low | 1 << distance
        if high != low and high < count:
            route += [(low, high), (high, low)]
    return lax.ppermute(block, axis, route)


def shifted(block, axis, distance):
    devices = range(lax.axis_size(axis))
    route = [(i - distance, i) for i in devices if i - distance in devices]
    return lax.ppermute(block, axis, route)


def padded_2(cells, sides, width):
    for axis, dim in sides:
        count = lax.axis_size(axis)
        ends = count - 1
        head = lax.slice_in_dim(cells, 0, width, axis=dim)
        tail = lax.slice_in_dim(cells, cells.shape[dim] - width, cells.shape[dim], axis=dim)
        cells = jnp.concatenate(
            [
                lax.ppermute(tail, axis, [(i, (i + 1) % count) for i in range(ends)]),
                cells,
                lax.ppermute(head, axis, [((i + 1) % count, i) for i in range(ends)]),
            ],
            axis=dim,
        )
    return cells


def per_device(video, conv_weight, norm_gain, norm_bias):
    frames, height, width, channels = video.shape
    tm_count = lax.axis_size("tm")
    current = video.astype(jnp.float32)
    position = lax.axis_index("tm")
    for bit_number in range(3):
        partner = from_partner(current, "tm", bit_number)
        is_upper = position >> bit_number & 1 == 1
        current = jnp.where(
            is_upper, (partner - current) * inv_root, (current + partner) * inv_root
        )
    wavelet = current.astype(jnp.bfloat16)
    last_frames = wavelet[frames - 2 :]
    earlier = shifted(last_frames, "tm", 1)
    extended = jnp.concatenate([earlier, wavelet], axis=0)
    with_rows = padded_2(extended, (("rows", 1),), 1)
    padded = jnp.pad(with_rows, ((0, 0), (0, 0), (1, 1), (0, 0)))
    convolved = lax.conv_general_dilated(
        padded[None],
        conv_weight,
        (1, 1, 1),
        "VALID",
        dimension_numbers=("NDHWC", "DHWIO", "NDHWC"),
        preferred_element_type=jnp.float32,
    )[0]
    out_frames, out_height, out_width, out_channels = convolved.shape
    group_count = GROUPS
    groups = convolved.reshape(
        out_frames, out_height, out_width, group_count, out_channels // group_count
    )
    entries = float(
        out_frames
        * out_height
        * out_width
        * (out_channels // group_count)
        * tm_count
        * lax.axis_size("rows")
    )
    local_sums = jnp.sum(groups, axis=(0, 1, 2, 4))
    group_total = lax.psum(local_sums, ("tm", "rows"))
    group_mean = group_total / entries
    centered = groups - group_mean[:, None]
    squares = lax.psum(jnp.sum(centered * centered, axis=(0, 1, 2, 4)), ("tm", "rows"))
    variance = squares / entries
    normed = (centered / jnp.sqrt(variance + 1e-05)[:, None]).reshape(
        out_frames, out_height, out_width, out_channels
    )
    activated = jax.nn.silu(normed * norm_gain + norm_bias).astype(jnp.bfloat16)
    arranged = activated.reshape(
        out_frames, out_height // 2, 2, out_width // 2, 2, out_channels
    ).transpose(1, 3, 0, 2, 4, 5)
    arranged = arranged.reshape(out_height // 2, out_width // 2, out_frames, 4 * out_channels)
    return lax.all_to_all(arranged, "tm", split_axis=1, concat_axis=2, tiled=True)


def solution(mesh):
    placed = (P("tm", "rows", None, None), P(), P(), P())
    return jax.shard_map(
        per_device,
        mesh=mesh,
        in_specs=placed,
        out_specs=P("rows", "tm", None, None),
        check_vma=False,
    )
```

profile of v0, /device:TPU:0, one launch (start us, length us, event | category | flops | bytes accessed | tf_op | source)
XLA Modules:
  0.0 597.1 jit_solution(17662172223809165032)
XLA Ops:
  0.0 4.3 convert_element_type.12
  4.3 3.3 collective-permute-start
  7.5 90.9 %collective-permute-done = f32[8,8,128,128]{3,2,1,0:T(8,128)} collective-permute-done((f32[8,8,128,128]{3,2,1,0:T(8,128)}, f32[8,8,128,128]{3,2,1,0:T(8,128)}, u32[]{:S(2)}, u32[]{:S(2)}) %collective-permute-start) | collective-permute-done | bytes 4194336 | tf_op jit(solution)/shard_map/ppermute | solution.py:17
  98.4 5.9 multiply_select_fusion.1
  104.3 1.5 collective-permute-start.1
  105.9 90.2 %collective-permute-done.1 = f32[8,8,128,128]{3,2,1,0:T(8,128)} collective-permute-done((f32[8,8,128,128]{3,2,1,0:T(8,128)}, f32[8,8,128,128]{3,2,1,0:T(8,128)}, u32[]{:S(2)}, u32[]{:S(2)}) %collective-permute-start.1) | collective-permute-done | bytes 4194336 | tf_op jit(solution)/shard_map/ppermute | solution.py:17
  196.1 6.9 %multiply_select_fusion = f32[8,8,128,128]{3,2,1,0:T(8,128)} fusion(f32[8,8,128,128]{3,2,1,0:T(8,128)} %multiply_select_fusion.1, f32[8,8,128,128]{3,2,1,0:T(8,128)} %collective-permute-done.1, pred[]{:T(512)S(6)} %eq.10), kind=kLoop, calls=%fused_computation.15 | loop fusion | flops 5242880 | bytes 12582913 | tf_op jit(solution)/shard_map/jit(_where)/select_n | solution.py:51
  203.0 3.0 collective-permute-start.2
  206.1 89.3 %collective-permute-done.2 = f32[8,8,128,128]{3,2,1,0:T(8,128)} collective-permute-done((f32[8,8,128,128]{3,2,1,0:T(8,128)}, f32[8,8,128,128]{3,2,1,0:T(8,128)}, u32[]{:S(2)}, u32[]{:S(2)}) %collective-permute-start.2) | collective-permute-done | bytes 4194336 | tf_op jit(solution)/shard_map/ppermute | solution.py:17
  295.4 4.5 select_convert_fusion
  299.9 5.1 collective-permute-start.3
  305.1 8.4 %collective-permute-done.3 = bf16[2,8,128,128]{3,2,1,0:T(8,128)(2,1)S(1)} collective-permute-done((bf16[2,8,128,128]{3,2,1,0:T(8,128)(2,1)S(1)}, bf16[2,8,128,128]{3,2,1,0:T(8,128)(2,1)S(1)}, u32[]{:S(2)}, u32[]{:S(2)}) %collective-permute-start.3) | collective-permute-done | bytes 524320 | tf_op jit(solution)/shard_map/ppermute | solution.py:23
  313.5 1.3 collective-permute-start.4
  314.9 1.3 collective-permute-start.5
  316.2 3.1 collective-permute-done.5
  319.3 2.1 fusion.13
  321.4 2.0 pad.5
  323.4 6.9 %reshape.19 = bf16[10,10,1,8,17,128]{5,4,3,1,0,2:T(8,128)(2,1)} reshape(bf16[10,10,1,136,128]{4,3,1,0,2:T(8,128)(2,1)} %pad.5) | data formatting | bytes 6963200 | tf_op jit(solution)/shard_map/conv_general_dilated | solution.py:60
  330.4 3.0 copy.29
  333.5 19.0 %select_reduce_fusion.1 = (f32[256]{0:T(256)S(1)}, f32[8,8,8,17,256]{4,2,3,1,0:T(8,128)}) fusion(pred[8,17]{0,1:T(8,128)(4,1)S(1)} %copy-done.3, bf16[3,3,3,128,256]{4,3,2,1,0:T(8,128)(2,1)S(1)} %copy-done, bf16[10,10,1,7,2,128]{5,3,4,1,0,2:T(8,128)(2,1)S(1)} %slice.15, bf16[10,10,1,8,17,128]{5,3,4,1,0,2:T(8,128)(2,1)S(1)} %copy.29), kind=kOutput, calls=%fused_computation.3 | convolution fusion | flops 15419842560 | bytes 14523528 | tf_op jit(solution)/shard_map/conv_general_dilated | solution.py:60
  352.8 75.9 %psum.14 = f32[32]{0:T(128)S(1)} all-reduce(f32[32]{0:T(128)S(1)} %reduce_sum.25), channel_id=1, replica_groups=mesh['tm'=32,'rows'=4] {'tm','rows'}, use_global_device_ids=true, to_apply=%region_2.3 | all-reduce | flops 32 | bytes 256 | tf_op jit(solution)/shard_map/psum | solution.py:82
  428.9 6.3 %copy.30 = f32[8,8,8,17,256]{4,1,3,2,0:T(8,128)S(1)} copy(f32[8,8,8,17,256]{4,2,3,1,0:T(8,128)} %get-tuple-element.8) | data formatting | bytes 17825792 | tf_op jit(solution)/shard_map/conv_general_dilated | solution.py:60
  435.2 1.5 select_reduce_fusion
  436.8 4.1 slice.16
  440.9 0.1 reduce_sum.37
  441.0 11.5 %copy.31 = f32[8,8,1,128,256]{4,0,3,1,2:T(8,128)} copy(f32[8,8,1,128,256]{4,1,3,0,2:T(8,128)} %slice.16) | data formatting | bytes 16777216 | tf_op jit(solution)/shard_map/conv_general_dilated | solution.py:60
  452.5 62.4 %psum.15 = f32[32]{0:T(128)S(1)} all-reduce(f32[32]{0:T(128)S(1)} %reduce_sum.37), channel_id=1, replica_groups=mesh['tm'=32,'rows'=4] {'tm','rows'}, use_global_device_ids=true, to_apply=%region_5.6 | all-reduce | flops 32 | bytes 256 | tf_op jit(solution)/shard_map/psum | solution.py:85
  515.2 6.9 %fusion.5 = bf16[4,64,8,2,2,256]{5,1,4,3,0,2:T(8,128)(2,1)S(1)} fusion(f32[256]{0:T(256)S(1)} %copy-done.4, f32[256]{0:T(256)S(1)} %copy-done.5, f32[256]{0:T(256)S(1)} %div.28, f32[256]{0:T(256)S(1)} %sub.32, f32[8,4,2,64,2,256]{5,0,4,3,2,1:T(8,128)} %bitcast.27), kind=kLoop, calls=%fused_computation.17 | loop fusion | flops 18874368 | bytes 12587008 | tf_op jit(solution)/shard_map/transpose | solution.py:93
  522.0 6.4 %copy.37 = bf16[4,64,8,2,2,256]{5,4,3,2,0,1:T(2,128)(2,1)} copy(bf16[4,64,8,2,2,256]{5,1,4,3,0,2:T(8,128)(2,1)S(1)} %fusion.5) | data formatting | bytes 8388608 | tf_op jit(solution)/shard_map/reshape | solution.py:94
  528.4 7.7 %reshape.33 = bf16[4,64,8,1024]{3,2,0,1:T(8,128)(2,1)} reshape(bf16[4,64,8,2,2,256]{5,4,3,2,0,1:T(2,128)(2,1)} %copy.37) | data formatting | bytes 8388608 | tf_op jit(solution)/shard_map/reshape | solution.py:94
  536.1 58.5 %all_to_all.18 = bf16[4,64,8,1024]{3,2,0,1:T(8,128)(2,1)S(1)} all-to-all(bf16[4,64,8,1024]{3,2,0,1:T(8,128)(2,1)} %reshape.33), channel_id=1, replica_groups=mesh['tm'=32,'rows'=4] {'tm'}, dimensions={1} | all-to-all | bytes 8388608 | tf_op jit(solution)/shard_map/all_to_all | solution.py:95
  594.6 2.5 copy.52
  (25 shorter events, 0.8 us)
Async XLA Ops:
  0.0 333.5 %copy-start = (bf16[3,3,3,128,256]{4,3,2,1,0:T(8,128)(2,1)S(1)}, bf16[3,3,3,128,256]{4,3,2,1,0:T(8,128)(2,1)}, u32[]{:S(2)}) copy-start(bf16[3,3,3,128,256]{4,3,2,1,0:T(8,128)(2,1)} %param.5) | copy-start | bytes 5308420
  4.3 94.2 %collective-permute-start = (f32[8,8,128,128]{3,2,1,0:T(8,128)}, f32[8,8,128,128]{3,2,1,0:T(8,128)}, u32[]{:S(2)}, u32[]{:S(2)}) collective-permute-start(f32[8,8,128,128]{3,2,1,0:T(8,128)} %convert_element_type.12), channel_id=1, source_target_pairs={{0,4},{4,0},{8,12},{12,8},{16,20},{20,16},{24,28},{28,24},{32,36},... | collective-permute-start | bytes 12582920 | tf_op jit(solution)/shard_map/ppermute | solution.py:17
  104.3 91.8 %collective-permute-start.1 = (f32[8,8,128,128]{3,2,1,0:T(8,128)}, f32[8,8,128,128]{3,2,1,0:T(8,128)}, u32[]{:S(2)}, u32[]{:S(2)}) collective-permute-start(f32[8,8,128,128]{3,2,1,0:T(8,128)} %multiply_select_fusion.1), channel_id=1, source_target_pairs={{0,8},{8,0},{4,12},{12,4},{16,24},{24,16},{20,28},{28,20},{32,40},... | collective-permute-start | bytes 12582920 | tf_op jit(solution)/shard_map/ppermute | solution.py:17
  203.0 92.4 %collective-permute-start.2 = (f32[8,8,128,128]{3,2,1,0:T(8,128)}, f32[8,8,128,128]{3,2,1,0:T(8,128)}, u32[]{:S(2)}, u32[]{:S(2)}) collective-permute-start(f32[8,8,128,128]{3,2,1,0:T(8,128)} %multiply_select_fusion), channel_id=1, source_target_pairs={{0,16},{16,0},{4,20},{20,4},{8,24},{24,8},{12,28},{28,12},{32,48},... | collective-permute-start | bytes 12582920 | tf_op jit(solution)/shard_map/ppermute | solution.py:17
  299.9 13.5 %collective-permute-start.3 = (bf16[2,8,128,128]{3,2,1,0:T(8,128)(2,1)S(1)}, bf16[2,8,128,128]{3,2,1,0:T(8,128)(2,1)S(1)}, u32[]{:S(2)}, u32[]{:S(2)}) collective-permute-start(bf16[2,8,128,128]{3,2,1,0:T(8,128)(2,1)S(1)} %slice.14), channel_id=1, source_target_pairs={{0,4},{4,8},{8,12},{12,16},{16,20},{20,24},{24,28},{28,32},{32,36}... | collective-permute-start | bytes 1572872 | tf_op jit(solution)/shard_map/ppermute | solution.py:23
  313.5 2.6 collective-permute-start.4
  314.9 4.4 collective-permute-start.5
  330.4 3.2 copy-start.3
  428.8 6.4 %copy-start.2 = (f32[8,8,8,17,256]{4,2,3,1,0:T(8,128)S(1)}, f32[8,8,8,17,256]{4,2,3,1,0:T(8,128)}, u32[]{:S(2)}) copy-start(f32[8,8,8,17,256]{4,2,3,1,0:T(8,128)} %get-tuple-element.8) | copy-start | bytes 26738692
  441.0 74.1 %copy-start.4 = (f32[256]{0:T(256)S(1)}, f32[256]{0:T(256)}, u32[]{:S(2)}) copy-start(f32[256]{0:T(256)} %param.7) | copy-start | bytes 3076
  441.0 74.1 %copy-start.5 = (f32[256]{0:T(256)S(1)}, f32[256]{0:T(256)}, u32[]{:S(2)}) copy-start(f32[256]{0:T(256)} %param.6) | copy-start | bytes 3076
  594.6 2.5 copy-start.1
where the time goes:
time: 598 us; the launch traced here: 597 us
  waiting for transfers between devices  282 us (47%)
  blocking collectives  197 us (33%)
  local copies, waits for them, and re-layouts  51 us (9%)
  other arithmetic  32.4 us (5%)
  matrix products  19 us (3%)
  starting transfers between devices  15.6 us (3%)
    ppermute x3, waiting for transfers between devices, from_partner(): return lax.ppermute(block, axis, route)  270 us
    psum x1, blocking collectives, per_device(): group_total = lax.psum(local_sums, ('tm', 'rows'))  75.9 us
    psum x1, blocking collectives, per_device(): lax.psum(jnp.sum(centered * centered, axis=(0, 1, 2, 4)), ('tm', 'rows'))  62.4 us
    all_to_all x1, blocking collectives, per_device(): lax.all_to_all(arranged, 'tm', split_axis=1, concat_axis=2, tiled=True)  58.5 us
    conv_general_dilated x6, local copies, waits for them, and re-layouts, per_device(): lax.conv_general_dilated(padded[None], conv_weight, (1, 1, 1), 'VALID', d...  31.9 us
    conv_general_dilated x1, matrix products, per_device(): lax.conv_general_dilated(padded[None], conv_weight, (1, 1, 1), 'VALID', d...  19 us
    reshape x2, local copies, waits for them, and re-layouts, per_device(): arranged.reshape(out_height // 2, out_width // 2, out_frames, 4 * out_cha...  14.1 us
    select_n x2, other arithmetic, per_device(): jnp.where(is_upper, (partner - current) * inv_root, (current + partner) *...  12.8 us
  transfers between devices with their start and end apart: 6, of which 5 were waited for; matrix products, arithmetic and copies ran while one was open for 0% of the time, Pallas kernels for 0%

commit v1 on v0

--- a/solution.py
+++ b/solution.py
@@ -79,7 +79,7 @@
         * lax.axis_size("rows")
     )
     local_sums = jnp.sum(groups, axis=(0, 1, 2, 4))
-    group_total = lax.psum(local_sums, ("tm", "rows"))
+    group_total = lax.psum(lax.psum(local_sums, "tm"), "rows")
     group_mean = group_total / entries
     centered = groups - group_mean[:, None]
     squares = lax.psum(jnp.sum(centered * centered, axis=(0, 1, 2, 4)), ("tm", "rows"))

time: 598 us -> 630 us (1.054)
  blocking collectives: 197 us -> 229 us
    psum x1 -> x2, blocking collectives: 75.9 us -> 107 us  [per_device(): group_total = lax.psum(lax.psum(local_sums, 'tm'), 'rows')]
where the time goes in v1:
time: 630 us; the launch traced here: 629 us
  waiting for transfers between devices  282 us (45%)
  blocking collectives  229 us (36%)
  local copies, waits for them, and re-layouts  51 us (8%)
  other arithmetic  32.4 us (5%)
  matrix products  19 us (3%)
  starting transfers between devices  15.6 us (2%)
    ppermute x3, waiting for transfers between devices, from_partner(): return lax.ppermute(block, axis, route)  270 us
    psum x2, blocking collectives, per_device(): group_total = lax.psum(lax.psum(local_sums, 'tm'), 'rows')  107 us
    psum x1, blocking collectives, per_device(): lax.psum(jnp.sum(centered * centered, axis=(0, 1, 2, 4)), ('tm', 'rows'))  63.5 us
    all_to_all x1, blocking collectives, per_device(): lax.all_to_all(arranged, 'tm', split_axis=1, concat_axis=2, tiled=True)  58.5 us
    conv_general_dilated x6, local copies, waits for them, and re-layouts, per_device(): lax.conv_general_dilated(padded[None], conv_weight, (1, 1, 1), 'VALID', d...  31.9 us
    conv_general_dilated x1, matrix products, per_device(): lax.conv_general_dilated(padded[None], conv_weight, (1, 1, 1), 'VALID', d...  19 us
    reshape x2, local copies, waits for them, and re-layouts, per_device(): arranged.reshape(out_height // 2, out_width // 2, out_frames, 4 * out_cha...  14.1 us
    select_n x2, other arithmetic, per_device(): jnp.where(is_upper, (partner - current) * inv_root, (current + partner) *...  12.8 us
  transfers between devices with their start and end apart: 6, of which 5 were waited for; matrix products, arithmetic and copies ran while one was open for 0% of the time, Pallas kernels for 0%

profile of v1, /device:TPU:0, one launch (start us, length us, event | category | flops | bytes accessed | tf_op | source)
XLA Modules:
  0.0 629.5 jit_solution(13479316300600433015)
XLA Ops:
  0.0 4.3 convert_element_type.12
  4.3 3.3 collective-permute-start
  7.5 90.9 %collective-permute-done = f32[8,8,128,128]{3,2,1,0:T(8,128)} collective-permute-done((f32[8,8,128,128]{3,2,1,0:T(8,128)}, f32[8,8,128,128]{3,2,1,0:T(8,128)}, u32[]{:S(2)}, u32[]{:S(2)}) %collective-permute-start) | collective-permute-done | bytes 4194336 | tf_op jit(solution)/shard_map/ppermute | solution.py:17
  98.4 5.9 multiply_select_fusion.1
  104.3 1.5 collective-permute-start.1
  105.9 90.2 %collective-permute-done.1 = f32[8,8,128,128]{3,2,1,0:T(8,128)} collective-permute-done((f32[8,8,128,128]{3,2,1,0:T(8,128)}, f32[8,8,128,128]{3,2,1,0:T(8,128)}, u32[]{:S(2)}, u32[]{:S(2)}) %collective-permute-start.1) | collective-permute-done | bytes 4194336 | tf_op jit(solution)/shard_map/ppermute | solution.py:17
  196.1 6.9 %multiply_select_fusion = f32[8,8,128,128]{3,2,1,0:T(8,128)} fusion(f32[8,8,128,128]{3,2,1,0:T(8,128)} %multiply_select_fusion.1, f32[8,8,128,128]{3,2,1,0:T(8,128)} %collective-permute-done.1, pred[]{:T(512)S(6)} %eq.10), kind=kLoop, calls=%fused_computation.15 | loop fusion | flops 5242880 | bytes 12582913 | tf_op jit(solution)/shard_map/jit(_where)/select_n | solution.py:51
  203.0 3.0 collective-permute-start.2
  206.1 89.3 %collective-permute-done.2 = f32[8,8,128,128]{3,2,1,0:T(8,128)} collective-permute-done((f32[8,8,128,128]{3,2,1,0:T(8,128)}, f32[8,8,128,128]{3,2,1,0:T(8,128)}, u32[]{:S(2)}, u32[]{:S(2)}) %collective-permute-start.2) | collective-permute-done | bytes 4194336 | tf_op jit(solution)/shard_map/ppermute | solution.py:17
  295.4 4.5 select_convert_fusion
  299.9 5.1 collective-permute-start.3
  305.1 8.4 %collective-permute-done.3 = bf16[2,8,128,128]{3,2,1,0:T(8,128)(2,1)S(1)} collective-permute-done((bf16[2,8,128,128]{3,2,1,0:T(8,128)(2,1)S(1)}, bf16[2,8,128,128]{3,2,1,0:T(8,128)(2,1)S(1)}, u32[]{:S(2)}, u32[]{:S(2)}) %collective-permute-start.3) | collective-permute-done | bytes 524320 | tf_op jit(solution)/shard_map/ppermute | solution.py:23
  313.5 1.3 collective-permute-start.4
  314.9 1.3 collective-permute-start.5
  316.2 3.1 collective-permute-done.5
  319.3 2.1 fusion.13
  321.4 2.0 pad.5
  323.4 6.9 %reshape.19 = bf16[10,10,1,8,17,128]{5,4,3,1,0,2:T(8,128)(2,1)} reshape(bf16[10,10,1,136,128]{4,3,1,0,2:T(8,128)(2,1)} %pad.5) | data formatting | bytes 6963200 | tf_op jit(solution)/shard_map/conv_general_dilated | solution.py:60
  330.4 3.0 copy.29
  333.5 19.0 %select_reduce_fusion.1 = (f32[256]{0:T(256)S(1)}, f32[8,8,8,17,256]{4,2,3,1,0:T(8,128)}) fusion(pred[8,17]{0,1:T(8,128)(4,1)S(1)} %copy-done.3, bf16[3,3,3,128,256]{4,3,2,1,0:T(8,128)(2,1)S(1)} %copy-done, bf16[10,10,1,7,2,128]{5,3,4,1,0,2:T(8,128)(2,1)S(1)} %slice.15, bf16[10,10,1,8,17,128]{5,3,4,1,0,2:T(8,128)(2,1)S(1)} %copy.29), kind=kOutput, calls=%fused_computation.3 | convolution fusion | flops 15419842560 | bytes 14523528 | tf_op jit(solution)/shard_map/conv_general_dilated | solution.py:60
  352.8 99.1 %psum.21 = f32[32]{0:T(128)S(1)} all-reduce(f32[32]{0:T(128)S(1)} %reduce_sum.25), channel_id=1, replica_groups=mesh['tm'=32,'rows'=4] {'tm'}, use_global_device_ids=true, to_apply=%region_2.3 | all-reduce | flops 32 | bytes 256 | tf_op jit(solution)/shard_map/psum | solution.py:82
  451.9 8.2 %psum.22 = f32[32]{0:T(128)S(1)} all-reduce(f32[32]{0:T(128)S(1)} %psum.21), channel_id=1, replica_groups=mesh['tm'=32,'rows'=4] {'rows'}, use_global_device_ids=true, to_apply=%region_3.4 | all-reduce | flops 32 | bytes 256 | tf_op jit(solution)/shard_map/psum | solution.py:82
  460.3 6.3 %copy.30 = f32[8,8,8,17,256]{4,1,3,2,0:T(8,128)S(1)} copy(f32[8,8,8,17,256]{4,2,3,1,0:T(8,128)} %get-tuple-element.8) | data formatting | bytes 17825792 | tf_op jit(solution)/shard_map/conv_general_dilated | solution.py:60
  466.6 1.5 select_reduce_fusion
  468.2 4.1 slice.16
  472.5 11.5 %copy.31 = f32[8,8,1,128,256]{4,0,3,1,2:T(8,128)} copy(f32[8,8,1,128,256]{4,1,3,0,2:T(8,128)} %slice.16) | data formatting | bytes 16777216 | tf_op jit(solution)/shard_map/conv_general_dilated | solution.py:60
  483.9 63.5 %psum.23 = f32[32]{0:T(128)S(1)} all-reduce(f32[32]{0:T(128)S(1)} %reduce_sum.37), channel_id=1, replica_groups=mesh['tm'=32,'rows'=4] {'tm','rows'}, use_global_device_ids=true, to_apply=%region_6.7 | all-reduce | flops 32 | bytes 256 | tf_op jit(solution)/shard_map/psum | solution.py:85
  547.6 6.9 %fusion.5 = bf16[4,64,8,2,2,256]{5,1,4,3,0,2:T(8,128)(2,1)S(1)} fusion(f32[256]{0:T(256)S(1)} %copy-done.4, f32[256]{0:T(256)S(1)} %copy-done.5, f32[256]{0:T(256)S(1)} %div.28, f32[256]{0:T(256)S(1)} %sub.32, f32[8,4,2,64,2,256]{5,0,4,3,2,1:T(8,128)} %bitcast.27), kind=kLoop, calls=%fused_computation.17 | loop fusion | flops 18874368 | bytes 12587008 | tf_op jit(solution)/shard_map/transpose | solution.py:93
  554.5 6.4 %copy.37 = bf16[4,64,8,2,2,256]{5,4,3,2,0,1:T(2,128)(2,1)} copy(bf16[4,64,8,2,2,256]{5,1,4,3,0,2:T(8,128)(2,1)S(1)} %fusion.5) | data formatting | bytes 8388608 | tf_op jit(solution)/shard_map/reshape | solution.py:94
  560.8 7.7 %reshape.33 = bf16[4,64,8,1024]{3,2,0,1:T(8,128)(2,1)} reshape(bf16[4,64,8,2,2,256]{5,4,3,2,0,1:T(2,128)(2,1)} %copy.37) | data formatting | bytes 8388608 | tf_op jit(solution)/shard_map/reshape | solution.py:94
  568.5 58.5 %all_to_all.18 = bf16[4,64,8,1024]{3,2,0,1:T(8,128)(2,1)S(1)} all-to-all(bf16[4,64,8,1024]{3,2,0,1:T(8,128)(2,1)} %reshape.33), channel_id=1, replica_groups=mesh['tm'=32,'rows'=4] {'tm'}, dimensions={1} | all-to-all | bytes 8388608 | tf_op jit(solution)/shard_map/all_to_all | solution.py:95
  627.0 2.5 copy.52
  (26 shorter events, 1.0 us)
Async XLA Ops:
  0.0 333.5 %copy-start = (bf16[3,3,3,128,256]{4,3,2,1,0:T(8,128)(2,1)S(1)}, bf16[3,3,3,128,256]{4,3,2,1,0:T(8,128)(2,1)}, u32[]{:S(2)}) copy-start(bf16[3,3,3,128,256]{4,3,2,1,0:T(8,128)(2,1)} %param.5) | copy-start | bytes 5308420
  4.3 94.2 %collective-permute-start = (f32[8,8,128,128]{3,2,1,0:T(8,128)}, f32[8,8,128,128]{3,2,1,0:T(8,128)}, u32[]{:S(2)}, u32[]{:S(2)}) collective-permute-start(f32[8,8,128,128]{3,2,1,0:T(8,128)} %convert_element_type.12), channel_id=1, source_target_pairs={{0,4},{4,0},{8,12},{12,8},{16,20},{20,16},{24,28},{28,24},{32,36},... | collective-permute-start | bytes 12582920 | tf_op jit(solution)/shard_map/ppermute | solution.py:17
  104.3 91.8 %collective-permute-start.1 = (f32[8,8,128,128]{3,2,1,0:T(8,128)}, f32[8,8,128,128]{3,2,1,0:T(8,128)}, u32[]{:S(2)}, u32[]{:S(2)}) collective-permute-start(f32[8,8,128,128]{3,2,1,0:T(8,128)} %multiply_select_fusion.1), channel_id=1, source_target_pairs={{0,8},{8,0},{4,12},{12,4},{16,24},{24,16},{20,28},{28,20},{32,40},... | collective-permute-start | bytes 12582920 | tf_op jit(solution)/shard_map/ppermute | solution.py:17
  203.0 92.4 %collective-permute-start.2 = (f32[8,8,128,128]{3,2,1,0:T(8,128)}, f32[8,8,128,128]{3,2,1,0:T(8,128)}, u32[]{:S(2)}, u32[]{:S(2)}) collective-permute-start(f32[8,8,128,128]{3,2,1,0:T(8,128)} %multiply_select_fusion), channel_id=1, source_target_pairs={{0,16},{16,0},{4,20},{20,4},{8,24},{24,8},{12,28},{28,12},{32,48},... | collective-permute-start | bytes 12582920 | tf_op jit(solution)/shard_map/ppermute | solution.py:17
  299.9 13.5 %collective-permute-start.3 = (bf16[2,8,128,128]{3,2,1,0:T(8,128)(2,1)S(1)}, bf16[2,8,128,128]{3,2,1,0:T(8,128)(2,1)S(1)}, u32[]{:S(2)}, u32[]{:S(2)}) collective-permute-start(bf16[2,8,128,128]{3,2,1,0:T(8,128)(2,1)S(1)} %slice.14), channel_id=1, source_target_pairs={{0,4},{4,8},{8,12},{12,16},{16,20},{20,24},{24,28},{28,32},{32,36}... | collective-permute-start | bytes 1572872 | tf_op jit(solution)/shard_map/ppermute | solution.py:23
  313.5 2.6 collective-permute-start.4
  314.9 4.4 collective-permute-start.5
  330.4 3.2 copy-start.3
  460.3 6.4 %copy-start.2 = (f32[8,8,8,17,256]{4,2,3,1,0:T(8,128)S(1)}, f32[8,8,8,17,256]{4,2,3,1,0:T(8,128)}, u32[]{:S(2)}) copy-start(f32[8,8,8,17,256]{4,2,3,1,0:T(8,128)} %get-tuple-element.8) | copy-start | bytes 26738692
  472.4 75.1 %copy-start.4 = (f32[256]{0:T(256)S(1)}, f32[256]{0:T(256)}, u32[]{:S(2)}) copy-start(f32[256]{0:T(256)} %param.7) | copy-start | bytes 3076
  472.5 75.1 %copy-start.5 = (f32[256]{0:T(256)S(1)}, f32[256]{0:T(256)}, u32[]{:S(2)}) copy-start(f32[256]{0:T(256)} %param.6) | copy-start | bytes 3076
  627.0 2.5 copy-start.1
